TPU v7x, 128 devices: a whole 4x4x4 slice. The times are simulated.
128 devices in a mesh: patch: 32 (over x, z, core), grp: 4 (over y).
Axes of the slice: x: 4, y: 4, z: 4, core: 2. Of those that a mesh axis runs over, the one named last changes fastest.
Arguments:
- incident: float32 [16, 262144], P(None, ('patch', 'grp')), may hold values from -6 to 6
- self_term: float32 [262144], P(('patch', 'grp')), may hold values from 1 to 3
- near_field: bfloat16 [262144, 2304], P(('patch', 'grp')), may hold values from -0.125 to 0.125
- history: bfloat16 [8, 16, 262144], P(None, None, 'patch'), may hold values from -6 to 6
- ret_values: bfloat16 [32768, 128, 128], P(('patch', 'grp')), may hold values from -0.125 to 0.125
- slot_row: int32 [32768], P(('patch', 'grp')), may hold values from 0 to 15
- slot_col: int32 [32768], P(('patch', 'grp')), may hold values from 0 to 191
- slot_delay: int32 [32768], P(('patch', 'grp')), may hold values from 0 to 7
- live_count: int32 [128], P(('patch', 'grp')), may hold values from 32 to 256, as said below
Outputs:
- current: float32 [16, 262144], P(None, ('patch', 'grp'))
- newest: bfloat16 [16, 262144], P(None, 'patch')
Inputs may be any that keep to these rules, and one draw needn't show every extreme that they name: The first live_count[d] slots of shard d are live, the rest ignored; some shard has all 256 slots live.
All inputs are finite; a program needn't handle non-finite values.
Results may differ from a plain program's by a relative error of at most 0.0055.
Values may be sent and summed in bfloat16 or wider, within the bound.
No kernel may reach another device: no remote copies, remote signals or barrier semaphores. Data moves between devices by JAX's collectives and lax.ppermute only.
A program may use at most 128 MiB of HBM per device.

v0:
```python
import jax
import jax.numpy as jnp
from jax import lax
from jax.sharding import PartitionSpec as P

BLK = 128
DELAYS = 8
SWEEPS = 4
RB = 16
SLOTS = 256


def extended_2(block, sides, width):
    for axis, dim in sides:
        count = lax.axis_size(axis)
        forward = [(i, i + 1) for i in range(count - 1)]
        backward = [(target, source) for source, target in forward]
        low = lax.ppermute(
            lax.slice_in_dim(block, block.shape[dim] - width, None, axis=dim), axis, forward
        )
        high = lax.ppermute(lax.slice_in_dim(block, 0, width, axis=dim), axis, backward)
        block = jnp.concatenate([low, block, high], axis=dim)
    return block


def body(
    incident, self_term, near_field, history, ret_values, slot_row, slot_col, slot_delay, live_count
):
    waves = incident.shape[0]
    own_cols = incident.shape[1]
    group_idx = lax.axis_index("grp")
    window = extended_2(history, (("patch", 2),), history.shape[2])
    grouped = window.reshape(DELAYS, waves, window.shape[2] // BLK, BLK)
    limit = live_count[0]
    blocks = grouped[slot_delay, :, slot_col, :]
    prods = jnp.einsum("swj,sij->swi", blocks, ret_values, preferred_element_type=jnp.float32)
    alive = (jnp.arange(SLOTS, dtype=jnp.int32) < limit).astype(jnp.float32)
    onehot = (slot_row[None, :] == jnp.arange(RB, dtype=jnp.int32)[:, None]).astype(
        jnp.float32
    ) * alive[None, :]
    retarded = jnp.einsum("rs,swi->wri", onehot, prods, precision=lax.Precision.HIGHEST)
    rhs = incident - retarded.reshape(waves, own_cols)
    sweep_in = lax.dynamic_slice_in_dim(history[0], group_idx * own_cols, own_cols, 1)
    current = sweep_in.astype(jnp.float32)
    for sweep in range(SWEEPS):
        extended = extended_2(sweep_in, (("patch", 1),), BLK)
        coupling = lax.dot_general(
            extended, near_field, (((1,), (1,)), ((), ())), preferred_element_type=jnp.float32
        )
        current = (rhs - coupling) / self_term[None, :]
        sweep_in = current.astype(jnp.bfloat16)
    newest = lax.all_gather(sweep_in, "grp", axis=1, tiled=True)
    return (current, newest)


def solution(mesh):
    placed = (
        P(None, ("patch", "grp")),
        P(("patch", "grp")),
        P(("patch", "grp"), None),
        P(None, None, "patch"),
        P(("patch", "grp"), None, None),
        P(("patch", "grp")),
        P(("patch", "grp")),
        P(("patch", "grp")),
        P(("patch", "grp")),
    )
    return jax.shard_map(
        body,
        mesh=mesh,
        in_specs=placed,
        out_specs=(P(None, ("patch", "grp")), P(None, "patch")),
        check_vma=False,
    )
```

profile of v0, /device:TPU:6, one launch (start us, length us, event | category | flops | bytes accessed | tf_op | source)
XLA Modules:
  0.0 111.1 jit_solution(12761360910164445370)
XLA Ops:
  0.6 5.7 %collective-permute-start.1 = (bf16[8,16,8192]{2,1,0:T(8,128)(2,1)}, bf16[8,16,8192]{2,1,0:T(8,128)(2,1)S(1)}, u32[]{:S(2)}, u32[]{:S(2)}) collective-permute-start(bf16[8,16,8192]{2,1,0:T(8,128)(2,1)} %param.12), channel_id=1, source_target_pairs={{4,0},{8,4},{12,8},{16,12},{20,16},{24,20},{28,24},{32,28},{36,32}... | collective-permute-start | bytes 6291464 | tf_op jit(solution)/shard_map/ppermute | solution.py:21
  6.3 1.9 %collective-permute-start = (bf16[8,16,8192]{2,1,0:T(8,128)(2,1)}, bf16[8,16,8192]{2,1,0:T(8,128)(2,1)}, u32[]{:S(2)}, u32[]{:S(2)}) collective-permute-start(bf16[8,16,8192]{2,1,0:T(8,128)(2,1)} %param.12), channel_id=1, source_target_pairs={{0,4},{4,8},{8,12},{12,16},{16,20},{20,24},{24,28},{28,32},{32,36}... | collective-permute-start | bytes 6291464 | tf_op jit(solution)/shard_map/ppermute | solution.py:18
  8.2 1.0 slice.27
  9.2 5.8 %collective-permute-start.3 = (bf16[16,128]{1,0:T(8,128)(2,1)S(1)}, bf16[16,128]{1,0:T(8,128)(2,1)S(1)}, u32[]{:S(2)}, u32[]{:S(2)}) collective-permute-start(bf16[16,128]{1,0:T(8,128)(2,1)S(1)} %get-tuple-element.9), channel_id=1, source_target_pairs={{4,0},{8,4},{12,8},{16,12},{20,16},{24,20},{28,24},{32,28},{36,32}... | collective-permute-start | bytes 12296 | tf_op jit(solution)/shard_map/ppermute | solution.py:21
  15.0 1.9 %collective-permute-start.2 = (bf16[16,128]{1,0:T(8,128)(2,1)S(1)}, bf16[16,128]{1,0:T(8,128)(2,1)S(1)}, u32[]{:S(2)}, u32[]{:S(2)}) collective-permute-start(bf16[16,128]{1,0:T(8,128)(2,1)S(1)} %get-tuple-element.8), channel_id=1, source_target_pairs={{0,4},{4,8},{8,12},{12,16},{16,20},{20,24},{24,28},{28,32},{32,36}... | collective-permute-start | bytes 12296 | tf_op jit(solution)/shard_map/ppermute | solution.py:18
  17.6 0.7 fusion.36
  18.3 11.8 %collective-permute-done.1 = bf16[8,16,8192]{2,1,0:T(8,128)(2,1)S(1)} collective-permute-done((bf16[8,16,8192]{2,1,0:T(8,128)(2,1)}, bf16[8,16,8192]{2,1,0:T(8,128)(2,1)S(1)}, u32[]{:S(2)}, u32[]{:S(2)}) %collective-permute-start.1) | collective-permute-done | bytes 2097184 | tf_op jit(solution)/shard_map/ppermute | solution.py:21
  30.1 5.9 %collective-permute-done = bf16[8,16,8192]{2,1,0:T(8,128)(2,1)} collective-permute-done((bf16[8,16,8192]{2,1,0:T(8,128)(2,1)}, bf16[8,16,8192]{2,1,0:T(8,128)(2,1)}, u32[]{:S(2)}, u32[]{:S(2)}) %collective-permute-start) | collective-permute-done | bytes 2097184 | tf_op jit(solution)/shard_map/ppermute | solution.py:18
  36.1 7.2 %copy_bitcast_fusion = bf16[8,16,192,128]{3,1,2,0:T(8,128)(2,1)} fusion(bf16[8,16,8192]{2,1,0:T(8,128)(2,1)S(1)} %collective-permute-done.1, bf16[8,16,8192]{2,1,0:T(8,128)(2,1)} %param.12, bf16[8,16,8192]{2,1,0:T(8,128)(2,1)} %collective-permute-done), kind=kLoop, calls=%fused_computation.1 | loop fusion | flops 18874368 | bytes 12582912 | tf_op jit(solution)/shard_map/reshape | solution.py:33
  43.2 4.0 %gather_fusion = bf16[256,16,128]{2,1,0:T(8,128)(2,1)S(1)} fusion(bf16[8,16,192,128]{3,1,2,0:T(8,128)(2,1)} %copy_bitcast_fusion, s32[256]{0:T(256)S(1)} %fusion.36), kind=kCustom, calls=%fused_computation | custom fusion | bytes 2099200 | tf_op jit(solution)/shard_map/gather | solution.py:35
  47.2 0.0 copy-start.2
  47.3 0.0 slice-start
  47.3 6.9 %fusion.49 = f32[256,16,128]{2,1,0:T(8,128)S(1)} fusion(bf16[256,16,128]{2,1,0:T(8,128)(2,1)S(1)} %gather_fusion, bf16[256,128,128]{2,1,0:T(8,128)(2,1)} %param.13), kind=kOutput, calls=%fused_computation.62 | convolution fusion | flops 134217728 | bytes 11534336 | tf_op jit(solution)/shard_map/swj,sij->swi/dot_general | solution.py:36
  54.2 1.8 %fusion.7 = f32[16,128,16]{1,2,0:T(8,128)S(1)} fusion(f32[256,16,128]{2,1,0:T(8,128)S(1)} %fusion.49, f32[256]{0:T(256)S(1)} %compare_convert_fusion, s32[256]{0:T(256)S(1)} %copy-done.2), kind=kOutput, calls=%fused_computation.14 | convolution fusion | flops 100671488 | bytes 2230272 | tf_op jit(solution)/shard_map/rs,swi->wri/dot_general | solution.py:41
  56.0 0.0 copy-done.1
  56.0 0.1 bitcast_subtract_fusion
  56.0 0.0 slice-start.2
  56.1 6.3 %fusion.4 = bf16[16,2048]{1,0:T(8,128)(2,1)S(1)} fusion(f32[16,2048]{1,0:T(8,128)S(1)} %bitcast_subtract_fusion, bf16[2048,2304]{1,0:T(8,128)(2,1)} %param.11, bf16[16,128]{1,0:T(8,128)(2,1)S(1)} %collective-permute-done.3, bf16[16,2048]{1,0:T(8,128)(2,1)S(1)} %dynamic-slice_bitcast_fusion, bf16[16,128]{1,0:T(8,128)(2,1)S(1)} %collective-permute-done.2, ...), kind=kOutput, calls=%fused_computation.11 | convolution fusion | flops 151314432 | bytes 9715712 | tf_op jit(solution)/shard_map/dot_general | solution.py:47
  62.4 1.9 %collective-permute-start.5 = (bf16[16,128]{1,0:T(8,128)(2,1)S(1)}, bf16[16,128]{1,0:T(8,128)(2,1)S(1)}, u32[]{:S(2)}, u32[]{:S(2)}) collective-permute-start(bf16[16,128]{1,0:T(8,128)(2,1)S(1)} %get-tuple-element.7), channel_id=1, source_target_pairs={{4,0},{8,4},{12,8},{16,12},{20,16},{24,20},{28,24},{32,28},{36,32}... | collective-permute-start | bytes 12296 | tf_op jit(solution)/shard_map/ppermute | solution.py:21
  64.3 2.4 %collective-permute-start.4 = (bf16[16,128]{1,0:T(8,128)(2,1)S(1)}, bf16[16,128]{1,0:T(8,128)(2,1)S(1)}, u32[]{:S(2)}, u32[]{:S(2)}) collective-permute-start(bf16[16,128]{1,0:T(8,128)(2,1)S(1)} %get-tuple-element.6), channel_id=1, source_target_pairs={{0,4},{4,8},{8,12},{12,16},{16,20},{20,24},{24,28},{28,32},{32,36}... | collective-permute-start | bytes 12296 | tf_op jit(solution)/shard_map/ppermute | solution.py:18
  66.8 4.6 %collective-permute-done.4 = bf16[16,128]{1,0:T(8,128)(2,1)S(1)} collective-permute-done((bf16[16,128]{1,0:T(8,128)(2,1)S(1)}, bf16[16,128]{1,0:T(8,128)(2,1)S(1)}, u32[]{:S(2)}, u32[]{:S(2)}) %collective-permute-start.4) | collective-permute-done | bytes 4128 | tf_op jit(solution)/shard_map/ppermute | solution.py:18
  71.4 2.5 %fusion.5 = bf16[16,2048]{1,0:T(8,128)(2,1)S(1)} fusion(f32[16,2048]{1,0:T(8,128)S(1)} %bitcast_subtract_fusion, bf16[2048,2304]{1,0:T(8,128)(2,1)S(1)} %bitcast.23, bf16[16,128]{1,0:T(8,128)(2,1)S(1)} %collective-permute-done.5, bf16[16,2048]{1,0:T(8,128)(2,1)S(1)} %fusion.4, bf16[16,128]{1,0:T(8,128)(2,1)S(1)} %collective-permute-done.4, f32[2048]{0:T(1024)S(1)} %copy-done), kind=kOutput, calls=%fused_computation.12 | convolution fusion | flops 151314432 | bytes 9715712 | tf_op jit(solution)/shard_map/dot_general | solution.py:47
  73.9 1.9 %collective-permute-start.7 = (bf16[16,128]{1,0:T(8,128)(2,1)S(1)}, bf16[16,128]{1,0:T(8,128)(2,1)S(1)}, u32[]{:S(2)}, u32[]{:S(2)}) collective-permute-start(bf16[16,128]{1,0:T(8,128)(2,1)S(1)} %get-tuple-element.5), channel_id=1, source_target_pairs={{4,0},{8,4},{12,8},{16,12},{20,16},{24,20},{28,24},{32,28},{36,32}... | collective-permute-start | bytes 12296 | tf_op jit(solution)/shard_map/ppermute | solution.py:21
  75.9 2.4 %collective-permute-start.6 = (bf16[16,128]{1,0:T(8,128)(2,1)S(1)}, bf16[16,128]{1,0:T(8,128)(2,1)S(1)}, u32[]{:S(2)}, u32[]{:S(2)}) collective-permute-start(bf16[16,128]{1,0:T(8,128)(2,1)S(1)} %get-tuple-element.4), channel_id=1, source_target_pairs={{0,4},{4,8},{8,12},{12,16},{16,20},{20,24},{24,28},{28,32},{32,36}... | collective-permute-start | bytes 12296 | tf_op jit(solution)/shard_map/ppermute | solution.py:18
  78.3 4.6 %collective-permute-done.6 = bf16[16,128]{1,0:T(8,128)(2,1)S(1)} collective-permute-done((bf16[16,128]{1,0:T(8,128)(2,1)S(1)}, bf16[16,128]{1,0:T(8,128)(2,1)S(1)}, u32[]{:S(2)}, u32[]{:S(2)}) %collective-permute-start.6) | collective-permute-done | bytes 4128 | tf_op jit(solution)/shard_map/ppermute | solution.py:18
  82.9 2.5 %fusion.6 = bf16[16,2048]{1,0:T(8,128)(2,1)S(1)} fusion(f32[16,2048]{1,0:T(8,128)S(1)} %bitcast_subtract_fusion, bf16[2048,2304]{1,0:T(8,128)(2,1)S(1)} %bitcast.23, bf16[16,128]{1,0:T(8,128)(2,1)S(1)} %collective-permute-done.7, bf16[16,2048]{1,0:T(8,128)(2,1)S(1)} %fusion.5, bf16[16,128]{1,0:T(8,128)(2,1)S(1)} %collective-permute-done.6, f32[2048]{0:T(1024)S(1)} %copy-done), kind=kOutput, calls=%fused_computation.13 | convolution fusion | flops 151314432 | bytes 9715712 | tf_op jit(solution)/shard_map/dot_general | solution.py:47
  85.5 1.9 %collective-permute-start.9 = (bf16[16,128]{1,0:T(8,128)(2,1)S(1)}, bf16[16,128]{1,0:T(8,128)(2,1)S(1)}, u32[]{:S(2)}, u32[]{:S(2)}) collective-permute-start(bf16[16,128]{1,0:T(8,128)(2,1)S(1)} %get-tuple-element.3), channel_id=1, source_target_pairs={{4,0},{8,4},{12,8},{16,12},{20,16},{24,20},{28,24},{32,28},{36,32}... | collective-permute-start | bytes 12296 | tf_op jit(solution)/shard_map/ppermute | solution.py:21
  87.4 2.4 %collective-permute-start.8 = (bf16[16,128]{1,0:T(8,128)(2,1)S(1)}, bf16[16,128]{1,0:T(8,128)(2,1)S(1)}, u32[]{:S(2)}, u32[]{:S(2)}) collective-permute-start(bf16[16,128]{1,0:T(8,128)(2,1)S(1)} %get-tuple-element.2), channel_id=1, source_target_pairs={{0,4},{4,8},{8,12},{12,16},{16,20},{20,24},{24,28},{28,32},{32,36}... | collective-permute-start | bytes 12296 | tf_op jit(solution)/shard_map/ppermute | solution.py:18
  89.8 4.6 %collective-permute-done.8 = bf16[16,128]{1,0:T(8,128)(2,1)S(1)} collective-permute-done((bf16[16,128]{1,0:T(8,128)(2,1)S(1)}, bf16[16,128]{1,0:T(8,128)(2,1)S(1)}, u32[]{:S(2)}, u32[]{:S(2)}) %collective-permute-start.8) | collective-permute-done | bytes 4128 | tf_op jit(solution)/shard_map/ppermute | solution.py:18
  94.4 3.2 %fusion.48 = (bf16[16,2048]{1,0:T(8,128)(2,1)S(1)}, f32[16,2048]{1,0:T(8,128)}) fusion(f32[2048]{0:T(1024)S(1)} %copy-done, f32[16,2048]{1,0:T(8,128)S(1)} %bitcast_subtract_fusion, bf16[2048,2304]{1,0:T(8,128)(2,1)S(1)} %bitcast.23, bf16[16,128]{1,0:T(8,128)(2,1)S(1)} %collective-permute-done.9, bf16[16,2048]{1,0:T(8,128)(2,1)S(1)} %fusion.6, ...), kind=kOutput, calls=%fused_computation.61 | convolution fusion | flops 151314432 | bytes 9846784 | tf_op jit(solution)/shard_map/dot_general | solution.py:47
  97.6 12.8 %all_gather.3 = bf16[16,8192]{1,0:T(8,128)(2,1)S(1)} all-gather(bf16[16,2048]{1,0:T(8,128)(2,1)S(1)} %get-tuple-element.10), channel_id=1, replica_groups=mesh['patch'=32,'grp'=4] {'grp'}, dimensions={1}, use_global_device_ids=true | all-gather | bytes 327680 | tf_op jit(solution)/shard_map/all_gather | solution.py:52
  110.4 0.7 copy.21
  (20 shorter events, 0.1 us)
Async XLA Ops:
  0.6 29.5 %collective-permute-start.1 = (bf16[8,16,8192]{2,1,0:T(8,128)(2,1)}, bf16[8,16,8192]{2,1,0:T(8,128)(2,1)S(1)}, u32[]{:S(2)}, u32[]{:S(2)}) collective-permute-start(bf16[8,16,8192]{2,1,0:T(8,128)(2,1)} %param.12), channel_id=1, source_target_pairs={{4,0},{8,4},{12,8},{16,12},{20,16},{24,20},{28,24},{32,28},{36,32}... | collective-permute-start | bytes 6291464 | tf_op jit(solution)/shard_map/ppermute | solution.py:21
  6.3 29.8 %collective-permute-start = (bf16[8,16,8192]{2,1,0:T(8,128)(2,1)}, bf16[8,16,8192]{2,1,0:T(8,128)(2,1)}, u32[]{:S(2)}, u32[]{:S(2)}) collective-permute-start(bf16[8,16,8192]{2,1,0:T(8,128)(2,1)} %param.12), channel_id=1, source_target_pairs={{0,4},{4,8},{8,12},{12,16},{16,20},{20,24},{24,28},{28,32},{32,36}... | collective-permute-start | bytes 6291464 | tf_op jit(solution)/shard_map/ppermute | solution.py:18
  9.2 46.8 %collective-permute-start.3 = (bf16[16,128]{1,0:T(8,128)(2,1)S(1)}, bf16[16,128]{1,0:T(8,128)(2,1)S(1)}, u32[]{:S(2)}, u32[]{:S(2)}) collective-permute-start(bf16[16,128]{1,0:T(8,128)(2,1)S(1)} %get-tuple-element.9), channel_id=1, source_target_pairs={{4,0},{8,4},{12,8},{16,12},{20,16},{24,20},{28,24},{32,28},{36,32}... | collective-permute-start | bytes 12296 | tf_op jit(solution)/shard_map/ppermute | solution.py:21
  15.0 41.1 %collective-permute-start.2 = (bf16[16,128]{1,0:T(8,128)(2,1)S(1)}, bf16[16,128]{1,0:T(8,128)(2,1)S(1)}, u32[]{:S(2)}, u32[]{:S(2)}) collective-permute-start(bf16[16,128]{1,0:T(8,128)(2,1)S(1)} %get-tuple-element.8), channel_id=1, source_target_pairs={{0,4},{4,8},{8,12},{12,16},{16,20},{20,24},{24,28},{28,32},{32,36}... | collective-permute-start | bytes 12296 | tf_op jit(solution)/shard_map/ppermute | solution.py:18
  47.2 7.0 %copy-start.2 = (s32[256]{0:T(256)S(1)}, s32[256]{0:T(256)}, u32[]{:S(2)}) copy-start(s32[256]{0:T(256)} %param.14) | copy-start | bytes 3076
  47.3 8.7 %copy-start.1 = (f32[16,2048]{1,0:T(8,128)S(1)}, f32[16,2048]{1,0:T(8,128)}, u32[]{:S(2)}) copy-start(f32[16,2048]{1,0:T(8,128)} %param.9) | copy-start | bytes 393220
  47.3 8.8 %copy-start = (f32[2048]{0:T(1024)S(1)}, f32[2048]{0:T(1024)}, u32[]{:S(2)}) copy-start(f32[2048]{0:T(1024)} %param.10) | copy-start | bytes 24580
  47.3 24.1 %slice-start = ((s8[9437184]{0:T(1024)(128)(4,1)}), s8[4194304]{0:T(1024)(128)(4,1)S(1)}, s32[]{:S(2)}) async-start(s8[9437184]{0:T(1024)(128)(4,1)} %bitcast.22), calls=%async_computation | async-start | bytes 8388608
  47.3 24.1 %slice-start.1 = ((s8[9437184]{0:T(1024)(128)(4,1)}), s8[4194304]{0:T(1024)(128)(4,1)S(1)}, s32[]{:S(2)}) async-start(s8[9437184]{0:T(1024)(128)(4,1)} %bitcast.22), calls=%async_computation.1 | async-start | bytes 8388608
  56.0 15.3 %slice-start.2 = ((s8[9437184]{0:T(1024)(128)(4,1)}), s8[1048576]{0:T(1024)(128)(4,1)S(1)}, s32[]{:S(2)}) async-start(s8[9437184]{0:T(1024)(128)(4,1)} %bitcast.22), calls=%async_computation.2 | async-start | bytes 2097152
  62.4 4.3 %collective-permute-start.5 = (bf16[16,128]{1,0:T(8,128)(2,1)S(1)}, bf16[16,128]{1,0:T(8,128)(2,1)S(1)}, u32[]{:S(2)}, u32[]{:S(2)}) collective-permute-start(bf16[16,128]{1,0:T(8,128)(2,1)S(1)} %get-tuple-element.7), channel_id=1, source_target_pairs={{4,0},{8,4},{12,8},{16,12},{20,16},{24,20},{28,24},{32,28},{36,32}... | collective-permute-start | bytes 12296 | tf_op jit(solution)/shard_map/ppermute | solution.py:21
  64.3 7.0 %collective-permute-start.4 = (bf16[16,128]{1,0:T(8,128)(2,1)S(1)}, bf16[16,128]{1,0:T(8,128)(2,1)S(1)}, u32[]{:S(2)}, u32[]{:S(2)}) collective-permute-start(bf16[16,128]{1,0:T(8,128)(2,1)S(1)} %get-tuple-element.6), channel_id=1, source_target_pairs={{0,4},{4,8},{8,12},{12,16},{16,20},{20,24},{24,28},{28,32},{32,36}... | collective-permute-start | bytes 12296 | tf_op jit(solution)/shard_map/ppermute | solution.py:18
  73.9 4.3 %collective-permute-start.7 = (bf16[16,128]{1,0:T(8,128)(2,1)S(1)}, bf16[16,128]{1,0:T(8,128)(2,1)S(1)}, u32[]{:S(2)}, u32[]{:S(2)}) collective-permute-start(bf16[16,128]{1,0:T(8,128)(2,1)S(1)} %get-tuple-element.5), channel_id=1, source_target_pairs={{4,0},{8,4},{12,8},{16,12},{20,16},{24,20},{28,24},{32,28},{36,32}... | collective-permute-start | bytes 12296 | tf_op jit(solution)/shard_map/ppermute | solution.py:21
  75.9 7.0 %collective-permute-start.6 = (bf16[16,128]{1,0:T(8,128)(2,1)S(1)}, bf16[16,128]{1,0:T(8,128)(2,1)S(1)}, u32[]{:S(2)}, u32[]{:S(2)}) collective-permute-start(bf16[16,128]{1,0:T(8,128)(2,1)S(1)} %get-tuple-element.4), channel_id=1, source_target_pairs={{0,4},{4,8},{8,12},{12,16},{16,20},{20,24},{24,28},{28,32},{32,36}... | collective-permute-start | bytes 12296 | tf_op jit(solution)/shard_map/ppermute | solution.py:18
  85.5 4.3 %collective-permute-start.9 = (bf16[16,128]{1,0:T(8,128)(2,1)S(1)}, bf16[16,128]{1,0:T(8,128)(2,1)S(1)}, u32[]{:S(2)}, u32[]{:S(2)}) collective-permute-start(bf16[16,128]{1,0:T(8,128)(2,1)S(1)} %get-tuple-element.3), channel_id=1, source_target_pairs={{4,0},{8,4},{12,8},{16,12},{20,16},{24,20},{28,24},{32,28},{36,32}... | collective-permute-start | bytes 12296 | tf_op jit(solution)/shard_map/ppermute | solution.py:21
  87.4 7.0 %collective-permute-start.8 = (bf16[16,128]{1,0:T(8,128)(2,1)S(1)}, bf16[16,128]{1,0:T(8,128)(2,1)S(1)}, u32[]{:S(2)}, u32[]{:S(2)}) collective-permute-start(bf16[16,128]{1,0:T(8,128)(2,1)S(1)} %get-tuple-element.2), channel_id=1, source_target_pairs={{0,4},{4,8},{8,12},{12,16},{16,20},{20,24},{24,28},{28,32},{32,36}... | collective-permute-start | bytes 12296 | tf_op jit(solution)/shard_map/ppermute | solution.py:18
where the time goes:
time: 112 us; the launch traced here: 111 us
  waiting for transfers between devices  31.6 us (28%)
  starting transfers between devices  28.2 us (25%)
  matrix products  23.2 us (21%)
  blocking collectives  12.8 us (11%)
  other arithmetic  7.93 us (7%)
  local copies, waits for them, and re-layouts  5.77 us (5%)
  between operations  1.54 us (1%)
    ppermute x5, waiting for transfers between devices, extended_2(): lax.ppermute(lax.slice_in_dim(block, block.shape[dim] - width, None, axis...  19.8 us
    ppermute x5, starting transfers between devices, extended_2(): lax.ppermute(lax.slice_in_dim(block, 0, width, axis=dim), axis, backward)  17.2 us
    dot_general x4, matrix products, body(): lax.dot_general(extended, near_field, (((1,), (1,)), ((), ())), preferred...  14.6 us
    all_gather x1, blocking collectives, body(): newest = lax.all_gather(sweep_in, 'grp', axis=1, tiled=True)  12.8 us
    ppermute x5, waiting for transfers between devices, extended_2(): lax.ppermute(lax.slice_in_dim(block, 0, width, axis=dim), axis, backward)  11.9 us
    ppermute x5, starting transfers between devices, extended_2(): lax.ppermute(lax.slice_in_dim(block, block.shape[dim] - width, None, axis...  11.1 us
    reshape x1, other arithmetic, body(): grouped = window.reshape(DELAYS, waves, window.shape[2] // BLK, BLK)  7.16 us
    dot_general x1, matrix products, body(): jnp.einsum('swj,sij->swi', blocks, ret_values, preferred_element_type=jnp...  6.91 us
  transfers between devices with their start and end apart: 10, of which 5 were waited for; matrix products, arithmetic and copies ran while one was open for 19% of the time, Pallas kernels for 0%

commit v1 on v0

--- a/solution.py
+++ b/solution.py
@@ -49,7 +49,10 @@
         )
         current = (rhs - coupling) / self_term[None, :]
         sweep_in = current.astype(jnp.bfloat16)
-    newest = lax.all_gather(sweep_in, "grp", axis=1, tiled=True)
+    count_2 = lax.axis_size("grp")
+    pieces = jnp.stack([sweep_in for _ in range(count_2)])
+    pieces = lax.all_to_all(pieces, "grp", split_axis=0, concat_axis=0)
+    newest = jnp.concatenate(pieces, axis=1)
     return (current, newest)
 
 

time: 112 us -> 110 us (0.982)
  blocking collectives: 12.8 us -> 10.9 us
    all_gather x1 -> x0, blocking collectives: 12.8 us -> none  [body(): newest = lax.all_gather(sweep_in, 'grp', axis=1, tiled=True)]
    all_to_all x0 -> x1, blocking collectives: none -> 10.9 us  [body(): pieces = lax.all_to_all(pieces, 'grp', split_axis=0, concat_axis=0)]
  transfers between devices with their start and end apart: 10 -> 10, of which waited for: 5 -> 5; matrix products, arithmetic and copies ran while one was open for 19% -> 20% of each run, Pallas kernels for 0% -> 0%
where the time goes in v1:
time: 110 us; the launch traced here: 109 us
  waiting for transfers between devices  31.6 us (29%)
  starting transfers between devices  28.2 us (26%)
  matrix products  23.2 us (21%)
  blocking collectives  10.9 us (10%)
  other arithmetic  7.93 us (7%)
  local copies, waits for them, and re-layouts  5.81 us (5%)
  between operations  1.54 us (1%)
    ppermute x5, waiting for transfers between devices, extended_2(): lax.ppermute(lax.slice_in_dim(block, block.shape[dim] - width, None, axis...  19.8 us
    ppermute x5, starting transfers between devices, extended_2(): lax.ppermute(lax.slice_in_dim(block, 0, width, axis=dim), axis, backward)  17.2 us
    dot_general x4, matrix products, body(): lax.dot_general(extended, near_field, (((1,), (1,)), ((), ())), preferred...  14.6 us
    ppermute x5, waiting for transfers between devices, extended_2(): lax.ppermute(lax.slice_in_dim(block, 0, width, axis=dim), axis, backward)  11.9 us
    ppermute x5, starting transfers between devices, extended_2(): lax.ppermute(lax.slice_in_dim(block, block.shape[dim] - width, None, axis...  11.1 us
    all_to_all x1, blocking collectives, body(): pieces = lax.all_to_all(pieces, 'grp', split_axis=0, concat_axis=0)  10.9 us
    reshape x1, other arithmetic, body(): grouped = window.reshape(DELAYS, waves, window.shape[2] // BLK, BLK)  7.16 us
    dot_general x1, matrix products, body(): jnp.einsum('swj,sij->swi', blocks, ret_values, preferred_element_type=jnp...  6.91 us
  transfers between devices with their start and end apart: 10, of which 5 were waited for; matrix products, arithmetic and copies ran while one was open for 20% of the time, Pallas kernels for 0%

profile of v1, /device:TPU:6, one launch (start us, length us, event | category | flops | bytes accessed | tf_op | source)
XLA Modules:
  0.0 109.3 jit_solution(15193734571890088657)
XLA Ops:
  0.6 5.7 %collective-permute-start.1 = (bf16[8,16,8192]{2,1,0:T(8,128)(2,1)}, bf16[8,16,8192]{2,1,0:T(8,128)(2,1)S(1)}, u32[]{:S(2)}, u32[]{:S(2)}) collective-permute-start(bf16[8,16,8192]{2,1,0:T(8,128)(2,1)} %param.12), channel_id=1, source_target_pairs={{4,0},{8,4},{12,8},{16,12},{20,16},{24,20},{28,24},{32,28},{36,32}... | collective-permute-start | bytes 6291464 | tf_op jit(solution)/shard_map/ppermute | solution.py:21
  6.3 1.9 %collective-permute-start = (bf16[8,16,8192]{2,1,0:T(8,128)(2,1)}, bf16[8,16,8192]{2,1,0:T(8,128)(2,1)}, u32[]{:S(2)}, u32[]{:S(2)}) collective-permute-start(bf16[8,16,8192]{2,1,0:T(8,128)(2,1)} %param.12), channel_id=1, source_target_pairs={{0,4},{4,8},{8,12},{12,16},{16,20},{20,24},{24,28},{28,32},{32,36}... | collective-permute-start | bytes 6291464 | tf_op jit(solution)/shard_map/ppermute | solution.py:18
  8.2 1.0 slice.27
  9.2 5.8 %collective-permute-start.3 = (bf16[16,128]{1,0:T(8,128)(2,1)S(1)}, bf16[16,128]{1,0:T(8,128)(2,1)S(1)}, u32[]{:S(2)}, u32[]{:S(2)}) collective-permute-start(bf16[16,128]{1,0:T(8,128)(2,1)S(1)} %get-tuple-element.9), channel_id=1, source_target_pairs={{4,0},{8,4},{12,8},{16,12},{20,16},{24,20},{28,24},{32,28},{36,32}... | collective-permute-start | bytes 12296 | tf_op jit(solution)/shard_map/ppermute | solution.py:21
  15.0 1.9 %collective-permute-start.2 = (bf16[16,128]{1,0:T(8,128)(2,1)S(1)}, bf16[16,128]{1,0:T(8,128)(2,1)S(1)}, u32[]{:S(2)}, u32[]{:S(2)}) collective-permute-start(bf16[16,128]{1,0:T(8,128)(2,1)S(1)} %get-tuple-element.8), channel_id=1, source_target_pairs={{0,4},{4,8},{8,12},{12,16},{16,20},{20,24},{24,28},{28,32},{32,36}... | collective-permute-start | bytes 12296 | tf_op jit(solution)/shard_map/ppermute | solution.py:18
  17.6 0.7 fusion.36
  18.3 11.8 %collective-permute-done.1 = bf16[8,16,8192]{2,1,0:T(8,128)(2,1)S(1)} collective-permute-done((bf16[8,16,8192]{2,1,0:T(8,128)(2,1)}, bf16[8,16,8192]{2,1,0:T(8,128)(2,1)S(1)}, u32[]{:S(2)}, u32[]{:S(2)}) %collective-permute-start.1) | collective-permute-done | bytes 2097184 | tf_op jit(solution)/shard_map/ppermute | solution.py:21
  30.1 5.9 %collective-permute-done = bf16[8,16,8192]{2,1,0:T(8,128)(2,1)} collective-permute-done((bf16[8,16,8192]{2,1,0:T(8,128)(2,1)}, bf16[8,16,8192]{2,1,0:T(8,128)(2,1)}, u32[]{:S(2)}, u32[]{:S(2)}) %collective-permute-start) | collective-permute-done | bytes 2097184 | tf_op jit(solution)/shard_map/ppermute | solution.py:18
  36.1 7.2 %copy_bitcast_fusion = bf16[8,16,192,128]{3,1,2,0:T(8,128)(2,1)} fusion(bf16[8,16,8192]{2,1,0:T(8,128)(2,1)S(1)} %collective-permute-done.1, bf16[8,16,8192]{2,1,0:T(8,128)(2,1)} %param.12, bf16[8,16,8192]{2,1,0:T(8,128)(2,1)} %collective-permute-done), kind=kLoop, calls=%fused_computation.1 | loop fusion | flops 18874368 | bytes 12582912 | tf_op jit(solution)/shard_map/reshape | solution.py:33
  43.2 4.0 %gather_fusion = bf16[256,16,128]{2,1,0:T(8,128)(2,1)S(1)} fusion(bf16[8,16,192,128]{3,1,2,0:T(8,128)(2,1)} %copy_bitcast_fusion, s32[256]{0:T(256)S(1)} %fusion.36), kind=kCustom, calls=%fused_computation | custom fusion | bytes 2099200 | tf_op jit(solution)/shard_map/gather | solution.py:35
  47.2 0.0 copy-start.2
  47.3 0.0 slice-start
  47.3 6.9 %fusion.49 = f32[256,16,128]{2,1,0:T(8,128)S(1)} fusion(bf16[256,16,128]{2,1,0:T(8,128)(2,1)S(1)} %gather_fusion, bf16[256,128,128]{2,1,0:T(8,128)(2,1)} %param.13), kind=kOutput, calls=%fused_computation.62 | convolution fusion | flops 134217728 | bytes 11534336 | tf_op jit(solution)/shard_map/swj,sij->swi/dot_general | solution.py:36
  54.2 1.8 %fusion.7 = f32[16,128,16]{1,2,0:T(8,128)S(1)} fusion(f32[256,16,128]{2,1,0:T(8,128)S(1)} %fusion.49, f32[256]{0:T(256)S(1)} %compare_convert_fusion, s32[256]{0:T(256)S(1)} %copy-done.2), kind=kOutput, calls=%fused_computation.14 | convolution fusion | flops 100671488 | bytes 2230272 | tf_op jit(solution)/shard_map/rs,swi->wri/dot_general | solution.py:41
  56.0 0.0 copy-done.1
  56.0 0.1 bitcast_subtract_fusion
  56.0 0.0 slice-start.2
  56.1 6.3 %fusion.4 = bf16[16,2048]{1,0:T(8,128)(2,1)S(1)} fusion(f32[16,2048]{1,0:T(8,128)S(1)} %bitcast_subtract_fusion, bf16[2048,2304]{1,0:T(8,128)(2,1)} %param.11, bf16[16,128]{1,0:T(8,128)(2,1)S(1)} %collective-permute-done.3, bf16[16,2048]{1,0:T(8,128)(2,1)S(1)} %dynamic-slice_bitcast_fusion, bf16[16,128]{1,0:T(8,128)(2,1)S(1)} %collective-permute-done.2, ...), kind=kOutput, calls=%fused_computation.11 | convolution fusion | flops 151314432 | bytes 9715712 | tf_op jit(solution)/shard_map/dot_general | solution.py:47
  62.4 1.9 %collective-permute-start.5 = (bf16[16,128]{1,0:T(8,128)(2,1)S(1)}, bf16[16,128]{1,0:T(8,128)(2,1)S(1)}, u32[]{:S(2)}, u32[]{:S(2)}) collective-permute-start(bf16[16,128]{1,0:T(8,128)(2,1)S(1)} %get-tuple-element.7), channel_id=1, source_target_pairs={{4,0},{8,4},{12,8},{16,12},{20,16},{24,20},{28,24},{32,28},{36,32}... | collective-permute-start | bytes 12296 | tf_op jit(solution)/shard_map/ppermute | solution.py:21
  64.3 2.4 %collective-permute-start.4 = (bf16[16,128]{1,0:T(8,128)(2,1)S(1)}, bf16[16,128]{1,0:T(8,128)(2,1)S(1)}, u32[]{:S(2)}, u32[]{:S(2)}) collective-permute-start(bf16[16,128]{1,0:T(8,128)(2,1)S(1)} %get-tuple-element.6), channel_id=1, source_target_pairs={{0,4},{4,8},{8,12},{12,16},{16,20},{20,24},{24,28},{28,32},{32,36}... | collective-permute-start | bytes 12296 | tf_op jit(solution)/shard_map/ppermute | solution.py:18
  66.8 4.6 %collective-permute-done.4 = bf16[16,128]{1,0:T(8,128)(2,1)S(1)} collective-permute-done((bf16[16,128]{1,0:T(8,128)(2,1)S(1)}, bf16[16,128]{1,0:T(8,128)(2,1)S(1)}, u32[]{:S(2)}, u32[]{:S(2)}) %collective-permute-start.4) | collective-permute-done | bytes 4128 | tf_op jit(solution)/shard_map/ppermute | solution.py:18
  71.4 2.5 %fusion.5 = bf16[16,2048]{1,0:T(8,128)(2,1)S(1)} fusion(f32[16,2048]{1,0:T(8,128)S(1)} %bitcast_subtract_fusion, bf16[2048,2304]{1,0:T(8,128)(2,1)S(1)} %bitcast.26, bf16[16,128]{1,0:T(8,128)(2,1)S(1)} %collective-permute-done.5, bf16[16,2048]{1,0:T(8,128)(2,1)S(1)} %fusion.4, bf16[16,128]{1,0:T(8,128)(2,1)S(1)} %collective-permute-done.4, f32[2048]{0:T(1024)S(1)} %copy-done), kind=kOutput, calls=%fused_computation.12 | convolution fusion | flops 151314432 | bytes 9715712 | tf_op jit(solution)/shard_map/dot_general | solution.py:47
  73.9 1.9 %collective-permute-start.7 = (bf16[16,128]{1,0:T(8,128)(2,1)S(1)}, bf16[16,128]{1,0:T(8,128)(2,1)S(1)}, u32[]{:S(2)}, u32[]{:S(2)}) collective-permute-start(bf16[16,128]{1,0:T(8,128)(2,1)S(1)} %get-tuple-element.5), channel_id=1, source_target_pairs={{4,0},{8,4},{12,8},{16,12},{20,16},{24,20},{28,24},{32,28},{36,32}... | collective-permute-start | bytes 12296 | tf_op jit(solution)/shard_map/ppermute | solution.py:21
  75.9 2.4 %collective-permute-start.6 = (bf16[16,128]{1,0:T(8,128)(2,1)S(1)}, bf16[16,128]{1,0:T(8,128)(2,1)S(1)}, u32[]{:S(2)}, u32[]{:S(2)}) collective-permute-start(bf16[16,128]{1,0:T(8,128)(2,1)S(1)} %get-tuple-element.4), channel_id=1, source_target_pairs={{0,4},{4,8},{8,12},{12,16},{16,20},{20,24},{24,28},{28,32},{32,36}... | collective-permute-start | bytes 12296 | tf_op jit(solution)/shard_map/ppermute | solution.py:18
  78.3 4.6 %collective-permute-done.6 = bf16[16,128]{1,0:T(8,128)(2,1)S(1)} collective-permute-done((bf16[16,128]{1,0:T(8,128)(2,1)S(1)}, bf16[16,128]{1,0:T(8,128)(2,1)S(1)}, u32[]{:S(2)}, u32[]{:S(2)}) %collective-permute-start.6) | collective-permute-done | bytes 4128 | tf_op jit(solution)/shard_map/ppermute | solution.py:18
  82.9 2.5 %fusion.6 = bf16[16,2048]{1,0:T(8,128)(2,1)S(1)} fusion(f32[16,2048]{1,0:T(8,128)S(1)} %bitcast_subtract_fusion, bf16[2048,2304]{1,0:T(8,128)(2,1)S(1)} %bitcast.26, bf16[16,128]{1,0:T(8,128)(2,1)S(1)} %collective-permute-done.7, bf16[16,2048]{1,0:T(8,128)(2,1)S(1)} %fusion.5, bf16[16,128]{1,0:T(8,128)(2,1)S(1)} %collective-permute-done.6, f32[2048]{0:T(1024)S(1)} %copy-done), kind=kOutput, calls=%fused_computation.13 | convolution fusion | flops 151314432 | bytes 9715712 | tf_op jit(solution)/shard_map/dot_general | solution.py:47
  85.5 1.9 %collective-permute-start.9 = (bf16[16,128]{1,0:T(8,128)(2,1)S(1)}, bf16[16,128]{1,0:T(8,128)(2,1)S(1)}, u32[]{:S(2)}, u32[]{:S(2)}) collective-permute-start(bf16[16,128]{1,0:T(8,128)(2,1)S(1)} %get-tuple-element.3), channel_id=1, source_target_pairs={{4,0},{8,4},{12,8},{16,12},{20,16},{24,20},{28,24},{32,28},{36,32}... | collective-permute-start | bytes 12296 | tf_op jit(solution)/shard_map/ppermute | solution.py:21
  87.4 2.4 %collective-permute-start.8 = (bf16[16,128]{1,0:T(8,128)(2,1)S(1)}, bf16[16,128]{1,0:T(8,128)(2,1)S(1)}, u32[]{:S(2)}, u32[]{:S(2)}) collective-permute-start(bf16[16,128]{1,0:T(8,128)(2,1)S(1)} %get-tuple-element.2), channel_id=1, source_target_pairs={{0,4},{4,8},{8,12},{12,16},{16,20},{20,24},{24,28},{28,32},{32,36}... | collective-permute-start | bytes 12296 | tf_op jit(solution)/shard_map/ppermute | solution.py:18
  89.8 4.6 %collective-permute-done.8 = bf16[16,128]{1,0:T(8,128)(2,1)S(1)} collective-permute-done((bf16[16,128]{1,0:T(8,128)(2,1)S(1)}, bf16[16,128]{1,0:T(8,128)(2,1)S(1)}, u32[]{:S(2)}, u32[]{:S(2)}) %collective-permute-start.8) | collective-permute-done | bytes 4128 | tf_op jit(solution)/shard_map/ppermute | solution.py:18
  94.4 3.2 %fusion.48 = (bf16[16,2048]{1,0:T(8,128)(2,1)S(1)}, f32[16,2048]{1,0:T(8,128)}) fusion(f32[2048]{0:T(1024)S(1)} %copy-done, f32[16,2048]{1,0:T(8,128)S(1)} %bitcast_subtract_fusion, bf16[2048,2304]{1,0:T(8,128)(2,1)S(1)} %bitcast.26, bf16[16,128]{1,0:T(8,128)(2,1)S(1)} %collective-permute-done.9, bf16[16,2048]{1,0:T(8,128)(2,1)S(1)} %fusion.6, ...), kind=kOutput, calls=%fused_computation.61 | convolution fusion | flops 151314432 | bytes 9846784 | tf_op jit(solution)/shard_map/dot_general | solution.py:47
  97.6 10.9 %all_to_all.5 = bf16[4,16,2048]{2,1,0:T(8,128)(2,1)S(1)} all-to-all(bf16[4,16,2048]{2,1,0:T(8,128)(2,1)S(1)} %stack.2), channel_id=1, replica_groups=mesh['patch'=32,'grp'=4] {'grp'}, dimensions={0} | all-to-all | bytes 524288 | tf_op jit(solution)/shard_map/all_to_all | solution.py:54
  108.6 0.7 copy.19
  (21 shorter events, 0.1 us)
Async XLA Ops:
  0.6 29.5 %collective-permute-start.1 = (bf16[8,16,8192]{2,1,0:T(8,128)(2,1)}, bf16[8,16,8192]{2,1,0:T(8,128)(2,1)S(1)}, u32[]{:S(2)}, u32[]{:S(2)}) collective-permute-start(bf16[8,16,8192]{2,1,0:T(8,128)(2,1)} %param.12), channel_id=1, source_target_pairs={{4,0},{8,4},{12,8},{16,12},{20,16},{24,20},{28,24},{32,28},{36,32}... | collective-permute-start | bytes 6291464 | tf_op jit(solution)/shard_map/ppermute | solution.py:21
  6.3 29.8 %collective-permute-start = (bf16[8,16,8192]{2,1,0:T(8,128)(2,1)}, bf16[8,16,8192]{2,1,0:T(8,128)(2,1)}, u32[]{:S(2)}, u32[]{:S(2)}) collective-permute-start(bf16[8,16,8192]{2,1,0:T(8,128)(2,1)} %param.12), channel_id=1, source_target_pairs={{0,4},{4,8},{8,12},{12,16},{16,20},{20,24},{24,28},{28,32},{32,36}... | collective-permute-start | bytes 6291464 | tf_op jit(solution)/shard_map/ppermute | solution.py:18
  9.2 46.8 %collective-permute-start.3 = (bf16[16,128]{1,0:T(8,128)(2,1)S(1)}, bf16[16,128]{1,0:T(8,128)(2,1)S(1)}, u32[]{:S(2)}, u32[]{:S(2)}) collective-permute-start(bf16[16,128]{1,0:T(8,128)(2,1)S(1)} %get-tuple-element.9), channel_id=1, source_target_pairs={{4,0},{8,4},{12,8},{16,12},{20,16},{24,20},{28,24},{32,28},{36,32}... | collective-permute-start | bytes 12296 | tf_op jit(solution)/shard_map/ppermute | solution.py:21
  15.0 41.1 %collective-permute-start.2 = (bf16[16,128]{1,0:T(8,128)(2,1)S(1)}, bf16[16,128]{1,0:T(8,128)(2,1)S(1)}, u32[]{:S(2)}, u32[]{:S(2)}) collective-permute-start(bf16[16,128]{1,0:T(8,128)(2,1)S(1)} %get-tuple-element.8), channel_id=1, source_target_pairs={{0,4},{4,8},{8,12},{12,16},{16,20},{20,24},{24,28},{28,32},{32,36}... | collective-permute-start | bytes 12296 | tf_op jit(solution)/shard_map/ppermute | solution.py:18
  47.2 7.0 %copy-start.2 = (s32[256]{0:T(256)S(1)}, s32[256]{0:T(256)}, u32[]{:S(2)}) copy-start(s32[256]{0:T(256)} %param.14) | copy-start | bytes 3076
  47.3 8.7 %copy-start.1 = (f32[16,2048]{1,0:T(8,128)S(1)}, f32[16,2048]{1,0:T(8,128)}, u32[]{:S(2)}) copy-start(f32[16,2048]{1,0:T(8,128)} %param.9) | copy-start | bytes 393220
  47.3 8.8 %copy-start = (f32[2048]{0:T(1024)S(1)}, f32[2048]{0:T(1024)}, u32[]{:S(2)}) copy-start(f32[2048]{0:T(1024)} %param.10) | copy-start | bytes 24580
  47.3 24.1 %slice-start = ((s8[9437184]{0:T(1024)(128)(4,1)}), s8[4194304]{0:T(1024)(128)(4,1)S(1)}, s32[]{:S(2)}) async-start(s8[9437184]{0:T(1024)(128)(4,1)} %bitcast.25), calls=%async_computation.1 | async-start | bytes 8388608
  47.3 24.1 %slice-start.1 = ((s8[9437184]{0:T(1024)(128)(4,1)}), s8[4194304]{0:T(1024)(128)(4,1)S(1)}, s32[]{:S(2)}) async-start(s8[9437184]{0:T(1024)(128)(4,1)} %bitcast.25), calls=%async_computation.2 | async-start | bytes 8388608
  56.0 15.3 %slice-start.2 = ((s8[9437184]{0:T(1024)(128)(4,1)}), s8[1048576]{0:T(1024)(128)(4,1)S(1)}, s32[]{:S(2)}) async-start(s8[9437184]{0:T(1024)(128)(4,1)} %bitcast.25), calls=%async_computation.3 | async-start | bytes 2097152
  62.4 4.3 %collective-permute-start.5 = (bf16[16,128]{1,0:T(8,128)(2,1)S(1)}, bf16[16,128]{1,0:T(8,128)(2,1)S(1)}, u32[]{:S(2)}, u32[]{:S(2)}) collective-permute-start(bf16[16,128]{1,0:T(8,128)(2,1)S(1)} %get-tuple-element.7), channel_id=1, source_target_pairs={{4,0},{8,4},{12,8},{16,12},{20,16},{24,20},{28,24},{32,28},{36,32}... | collective-permute-start | bytes 12296 | tf_op jit(solution)/shard_map/ppermute | solution.py:21
  64.3 7.0 %collective-permute-start.4 = (bf16[16,128]{1,0:T(8,128)(2,1)S(1)}, bf16[16,128]{1,0:T(8,128)(2,1)S(1)}, u32[]{:S(2)}, u32[]{:S(2)}) collective-permute-start(bf16[16,128]{1,0:T(8,128)(2,1)S(1)} %get-tuple-element.6), channel_id=1, source_target_pairs={{0,4},{4,8},{8,12},{12,16},{16,20},{20,24},{24,28},{28,32},{32,36}... | collective-permute-start | bytes 12296 | tf_op jit(solution)/shard_map/ppermute | solution.py:18
  73.9 4.3 %collective-permute-start.7 = (bf16[16,128]{1,0:T(8,128)(2,1)S(1)}, bf16[16,128]{1,0:T(8,128)(2,1)S(1)}, u32[]{:S(2)}, u32[]{:S(2)}) collective-permute-start(bf16[16,128]{1,0:T(8,128)(2,1)S(1)} %get-tuple-element.5), channel_id=1, source_target_pairs={{4,0},{8,4},{12,8},{16,12},{20,16},{24,20},{28,24},{32,28},{36,32}... | collective-permute-start | bytes 12296 | tf_op jit(solution)/shard_map/ppermute | solution.py:21
  75.9 7.0 %collective-permute-start.6 = (bf16[16,128]{1,0:T(8,128)(2,1)S(1)}, bf16[16,128]{1,0:T(8,128)(2,1)S(1)}, u32[]{:S(2)}, u32[]{:S(2)}) collective-permute-start(bf16[16,128]{1,0:T(8,128)(2,1)S(1)} %get-tuple-element.4), channel_id=1, source_target_pairs={{0,4},{4,8},{8,12},{12,16},{16,20},{20,24},{24,28},{28,32},{32,36}... | collective-permute-start | bytes 12296 | tf_op jit(solution)/shard_map/ppermute | solution.py:18
  85.5 4.3 %collective-permute-start.9 = (bf16[16,128]{1,0:T(8,128)(2,1)S(1)}, bf16[16,128]{1,0:T(8,128)(2,1)S(1)}, u32[]{:S(2)}, u32[]{:S(2)}) collective-permute-start(bf16[16,128]{1,0:T(8,128)(2,1)S(1)} %get-tuple-element.3), channel_id=1, source_target_pairs={{4,0},{8,4},{12,8},{16,12},{20,16},{24,20},{28,24},{32,28},{36,32}... | collective-permute-start | bytes 12296 | tf_op jit(solution)/shard_map/ppermute | solution.py:21
  87.4 7.0 %collective-permute-start.8 = (bf16[16,128]{1,0:T(8,128)(2,1)S(1)}, bf16[16,128]{1,0:T(8,128)(2,1)S(1)}, u32[]{:S(2)}, u32[]{:S(2)}) collective-permute-start(bf16[16,128]{1,0:T(8,128)(2,1)S(1)} %get-tuple-element.2), channel_id=1, source_target_pairs={{0,4},{4,8},{8,12},{12,16},{16,20},{20,24},{24,28},{28,32},{32,36}... | collective-permute-start | bytes 12296 | tf_op jit(solution)/shard_map/ppermute | solution.py:18
